TPU v7x, 32 devices: a whole 2x2x4 slice. The times are simulated.
32 devices in a mesh: groups: 1, expert: 16 (over z, y, x), replica: 2 (over core).
Axes of the slice: x: 2, y: 2, z: 4, core: 2. Of those that a mesh axis runs over, the one named last changes fastest.
Arguments:
- hidden_rows: bfloat16 [1024, 3584], P(('groups', 'expert', 'replica')), may hold values from -6 to 6
- norm_gain: float32 [3584], replicated, may hold values from 0.5 to 1.5
- expert_ids: int32 [1024, 2], P(('groups', 'expert', 'replica')), may hold values from 0 to 3, all different within a row; in each aligned block of 32 rows (0 to 31, 32 to 63, ...) at most 32 rows name the same one
- capacity: int32 [4], replicated, may hold values from 16 to 32
- route_probs: float32 [1024, 2], P(('groups', 'expert', 'replica')), may hold values from 0.2 to 1
- w_gate: bfloat16 [16, 2, 3584, 304], P('expert', 'replica'), may hold values from -0.09375 to 0.09375
- w_up: bfloat16 [16, 2, 3584, 304], P('expert', 'replica'), may hold values from -0.09375 to 0.09375
- w_down: bfloat16 [16, 2, 304, 3584], P('expert', 'replica'), may hold values from -0.125 to 0.125
Outputs:
- moved: bfloat16 [1024, 3584], P(('groups', 'expert', 'replica'))
Inputs may be any that keep to these rules, and one draw needn't show every extreme that they name: `expert_ids`: in the 8 rows of one device no expert is named more than 32 times, a bound that some block reaches; the two ids of a row differ.
All inputs are finite; a program needn't handle non-finite values.
Results may differ from a plain program's by a relative error of at most 0.006.
Values may be sent and summed in bfloat16 or wider, within the bound.
A program may use at most 64 MiB of HBM per device.

v0:
```python
import jax
import jax.numpy as jnp
from jax import lax
from jax.sharding import PartitionSpec as P

TGROUP = 8


def serve_slots(received, w_gate, w_up, w_down):
    sources, count, model_width = received.shape
    flattened = received.reshape(sources * count, model_width)
    gate_out = jnp.dot(flattened, w_gate[0, 0], preferred_element_type=jnp.float32)
    up_out = jnp.dot(flattened, w_up[0, 0], preferred_element_type=jnp.float32)
    hidden = (jax.nn.silu(gate_out) * up_out).astype(jnp.bfloat16)
    pieces = jnp.dot(hidden, w_down[0, 0], preferred_element_type=jnp.float32).astype(jnp.bfloat16)
    return pieces.reshape(sources, count, model_width)


def per_device(hidden_rows, norm_gain, expert_ids, capacity, route_probs, w_gate, w_up, w_down):
    row_count, model_width = hidden_rows.shape
    lane_count = lax.axis_size("expert")
    copies = lax.axis_size("replica")
    families = lane_count // TGROUP
    experts = families * copies
    slot_count = min(row_count, max(TGROUP, 4 * row_count // experts))
    widened = hidden_rows.astype(jnp.float32)
    scaling = lax.rsqrt(jnp.mean(widened * widened, axis=-1, keepdims=True) + 1e-05)
    normed = (widened * scaling * norm_gain).astype(jnp.bfloat16)
    assigned = expert_ids.reshape(2 * row_count)
    labels = jnp.arange(experts, dtype=jnp.int32)
    onehot = (assigned[:, None] == labels[None, :]).astype(jnp.int32)
    order_iota = jnp.arange(2 * row_count, dtype=jnp.int32)
    earlier = (order_iota[None, :] < order_iota[:, None]).astype(jnp.float32)
    counted = jnp.dot(earlier, onehot.astype(jnp.float32), preferred_element_type=jnp.float32)
    slot_rank = jnp.sum(counted.astype(jnp.int32) * onehot, axis=1)
    cap_limit = jnp.sum(onehot * capacity[None, :], axis=1)
    keep_mask = (slot_rank < cap_limit).astype(jnp.int32)
    slot_iota = jnp.arange(slot_count, dtype=jnp.int32)
    chosen = onehot.T * keep_mask[None, :]
    selection = chosen[:, None, :] * (slot_rank[None, None, :] == slot_iota[None, :, None]).astype(
        jnp.int32
    )
    selection = selection.astype(jnp.float32).reshape(experts, slot_count, row_count, 2)
    sel_rows = jnp.sum(selection, axis=3)
    weights_rows = jnp.sum(selection * route_probs[None, None, :, :], axis=3)
    outgoing = jnp.einsum(
        "ecr,rd->ecd", sel_rows.astype(jnp.bfloat16), normed, preferred_element_type=jnp.float32
    ).astype(jnp.bfloat16)
    spread = jnp.broadcast_to(
        outgoing.reshape(families, 1, copies, slot_count, model_width),
        (families, TGROUP, copies, slot_count, model_width),
    ).reshape(lane_count * copies, slot_count, model_width)
    pieces = serve_slots(
        lax.all_to_all(spread, ("expert", "replica"), split_axis=0, concat_axis=0, tiled=True),
        w_gate,
        w_up,
        w_down,
    )
    returned = lax.all_to_all(
        pieces, ("expert", "replica"), split_axis=0, concat_axis=0, tiled=True
    )
    summed = (
        returned.reshape(families, TGROUP, copies, slot_count, model_width)
        .astype(jnp.float32)
        .sum(axis=1)
        .reshape(experts, slot_count, model_width)
    )
    mixture = jnp.einsum("ecr,ecd->rd", weights_rows, summed)
    return (widened + mixture).astype(jnp.bfloat16)


def solution(mesh):
    placed = (
        P(("groups", "expert", "replica"), None),
        P(),
        P(("groups", "expert", "replica"), None),
        P(),
        P(("groups", "expert", "replica"), None),
        P("expert", "replica", None, None),
        P("expert", "replica", None, None),
        P("expert", "replica", None, None),
    )
    return jax.shard_map(
        per_device,
        mesh=mesh,
        in_specs=placed,
        out_specs=P(("groups", "expert", "replica"), None),
        check_vma=False,
    )
```

profile of v0, /device:TPU:0, one launch (start us, length us, event | category | flops | bytes accessed | tf_op | source)
XLA Modules:
  0.0 351.2 jit_solution(9474088067206435548)
XLA Ops:
  0.0 0.0 copy-start
  0.0 1.2 fusion.15
  1.3 0.8 copy.15
  2.0 0.1 eq.47
  2.1 0.1 fusion.14
  2.3 0.8 select_reduce_fusion
  3.0 0.1 reduce_sum.59
  3.1 0.1 copy.17
  3.2 0.1 reduce_sum.61
  3.3 0.1 copy.16
  3.4 0.7 compare_select_fusion
  4.1 0.7 convert_reduce_fusion.1
  4.8 1.4 convolution_convert_fusion.1
  6.2 0.8 broadcast_in_dim.5
  7.1 0.0 copy-start.2
  7.1 168.2 %all_to_all.10 = bf16[32,32,3584]{2,1,0:T(8,128)(2,1)S(1)} all-to-all(bf16[32,32,3584]{2,1,0:T(8,128)(2,1)S(1)} %bitcast.35), channel_id=1, replica_groups=mesh['groups'=1,'expert'=16,'replica'=2] {'expert','replica'}, dimensions={0} | all-to-all | bytes 14680064 | tf_op jit(solution)/shard_map/all_to_all | solution.py:54
  175.2 0.0 copy-done.2
  175.2 2.4 fusion.5
  177.7 2.5 fusion.10
  180.2 0.0 copy-done
  180.2 4.3 %convolution_convert_fusion = bf16[1024,3584]{1,0:T(8,128)(2,1)S(1)} fusion(bf16[1024,304]{0,1:T(8,128)(2,1)S(1)} %fusion.10, bf16[1,1,304,3584]{3,2,1,0:T(8,128)(2,1)S(1)} %copy-done), kind=kOutput, calls=%fused_computation.1 | convolution fusion | flops 2235039744 | bytes 10141696 | tf_op jit(solution)/shard_map/dot_general | solution.py:15
  184.5 164.7 %all_to_all.11 = bf16[32,32,3584]{2,1,0:T(8,128)(2,1)S(1)} all-to-all(bf16[32,32,3584]{2,1,0:T(8,128)(2,1)S(1)} %bitcast.39), channel_id=1, replica_groups=mesh['groups'=1,'expert'=16,'replica'=2] {'expert','replica'}, dimensions={0} | all-to-all | bytes 14680064 | tf_op jit(solution)/shard_map/all_to_all | solution.py:59
  349.2 1.0 convert_reduce_fusion
  350.2 1.0 fusion.1
  (7 shorter events, 0.0 us)
Async XLA Ops:
  0.0 180.2 %copy-start = (bf16[1,1,304,3584]{3,2,1,0:T(8,128)(2,1)S(1)}, bf16[1,1,304,3584]{3,2,1,0:T(8,128)(2,1)}, u32[]{:S(2)}) copy-start(bf16[1,1,304,3584]{3,2,1,0:T(8,128)(2,1)} %param.15) | copy-start | bytes 6537220
  7.1 168.2 %copy-start.2 = (bf16[1,1,3584,304]{2,3,1,0:T(8,128)(2,1)S(1)}, bf16[1,1,3584,304]{2,3,1,0:T(8,128)(2,1)}, u32[]{:S(2)}) copy-start(bf16[1,1,3584,304]{2,3,1,0:T(8,128)(2,1)} %param.13) | copy-start | bytes 6537220
  175.2 2.4 copy-start.3
  349.2 1.0 copy-start.1
where the time goes:
time: 351 us
  blocking collectives  333 us (95%)
  matrix products  11.7 us (3%)
  other arithmetic  4.4 us (1%)
    all_to_all x1, blocking collectives, per_device(): lax.all_to_all(spread, ('expert', 'replica'), split_axis=0, concat_axis=0...  168 us
    all_to_all x1, blocking collectives, per_device(): lax.all_to_all(pieces, ('expert', 'replica'), split_axis=0, concat_axis=0...  165 us

commit v1 on v0

--- a/solution.py
+++ b/solution.py
@@ -1,6 +1,8 @@
 import jax
 import jax.numpy as jnp
 from jax import lax
+from jax.experimental import pallas as pl
+from jax.experimental.pallas import tpu as pltpu
 from jax.sharding import PartitionSpec as P
 
 TGROUP = 8
@@ -69,6 +71,268 @@
     return (widened + mixture).astype(jnp.bfloat16)
 
 
+CHAIN = 4
+LANES = 128
+HALF = 16
+BLOCK = 2 * HALF
+SIDE = CHAIN * BLOCK
+BATCH = 2 * SIDE
+STEP = 512
+
+
+def rows_at(dc, dz, h=None):
+    start = dc * SIDE + dz * BLOCK
+    return pl.ds(start, BLOCK) if h is None else pl.ds(start + h * HALF, HALF)
+
+
+def layer_kernel(
+    hidden_ref, gain_ref, ids_ref, cap_ref, probs_ref, wg_hbm, wu_hbm, wd_hbm, out_ref,
+    rows_buf, part_buf, pair_buf, far_buf, near_buf, chain_buf, wg, wu, wd, acc_g, acc_u, hid,
+    load_sem, send_sem, recv_sem,
+):
+    width = hidden_ref.shape[1]
+    experts = cap_ref.shape[0]
+    me = lax.axis_index("expert")
+    core = lax.axis_index("replica")
+    total = lax.axis_size("expert")
+    x_side = {"expert": me + 1 - 2 * lax.rem(me, 2)}
+    y_side = {"expert": me + 2 - 4 * lax.rem(lax.div(me, 2), 2)}
+    sibling = {"replica": 1 - core}
+    along = [{"expert": lax.rem(me + 4 * k, total)} for k in range(CHAIN)]
+    near = (x_side, y_side)
+    far = (y_side, x_side)
+
+    loads = [
+        pltpu.make_async_copy(src, dst, load_sem.at[n])
+        for n, (src, dst) in enumerate(((wg_hbm, wg), (wu_hbm, wu), (wd_hbm, wd)))
+    ]
+    for load in loads:
+        load.start()
+
+    barrier = pltpu.get_barrier_semaphore()
+    partners = [x_side, y_side, sibling] + along[1:]
+    for partner in partners:
+        pl.semaphore_signal(barrier, inc=1, device_id=partner, device_id_type=pl.DeviceIdType.MESH)
+
+    widened = hidden_ref[...].astype(jnp.float32)
+    scaling = lax.rsqrt(jnp.mean(widened * widened, axis=-1, keepdims=True) + 1e-05)
+    rows_buf[0, pl.ds(0, BLOCK), pl.ds(0, width)] = (widened * scaling * gain_ref[...]).astype(jnp.bfloat16)
+    lane = lax.broadcasted_iota(jnp.int32, (BLOCK, LANES), 1)
+    label = jnp.where(lane < LANES // 2, lane, lane - LANES // 2)
+    first = ids_ref[:, 0:1] == label
+    second = ids_ref[:, 1:2] == label
+    named = jnp.where(first | second, 1.0, 0.0)
+    earlier = lax.broadcasted_iota(jnp.int32, (BLOCK, BLOCK), 1) < lax.broadcasted_iota(jnp.int32, (BLOCK, BLOCK), 0)
+    rank = jnp.dot(
+        jnp.where(earlier, 1.0, 0.0).astype(jnp.bfloat16),
+        named.astype(jnp.bfloat16),
+        preferred_element_type=jnp.float32,
+    )
+    limit = jnp.zeros((BLOCK, LANES), jnp.float32)
+    for e in range(experts):
+        limit = jnp.where(label == e, cap_ref[e].astype(jnp.float32), limit)
+    weight = jnp.where(first, probs_ref[:, 0:1], 0.0) + jnp.where(second, probs_ref[:, 1:2], 0.0)
+    weight = jnp.where(rank < limit, weight, 0.0)
+    high = weight.astype(jnp.bfloat16).astype(jnp.float32)
+    rows_buf[0, pl.ds(0, BLOCK), pl.ds(width, LANES)] = jnp.where(
+        lane < LANES // 2, high, weight - high
+    ).astype(jnp.bfloat16)
+
+    pl.semaphore_wait(barrier, len(partners))
+
+    sent = {}
+
+    def send(name, src, dst, device):
+        n = len(sent)
+        copy = pltpu.make_async_remote_copy(
+            src_ref=src, dst_ref=dst, send_sem=send_sem.at[n], recv_sem=recv_sem.at[n],
+            device_id=device, device_id_type=pl.DeviceIdType.MESH,
+        )
+        copy.start()
+        sent[name] = copy
+
+    def to_near(dz):
+        for h in range(2):
+            send(("near", dz, h), rows_buf.at[0, rows_at(0, dz, h)], rows_buf.at[1, rows_at(0, dz, h)], near[h])
+
+    def to_far(b, dz):
+        for h in range(2):
+            send(("far", b, dz, h), rows_buf.at[b, rows_at(0, dz, h)], rows_buf.at[2 + b, rows_at(0, dz, h)], far[h])
+
+    def to_sibling(batch, dz):
+        send(("pair", batch, dz), rows_buf.at[batch, rows_at(0, dz)], rows_buf.at[batch, rows_at(1, dz)], sibling)
+
+    def got(*name):
+        sent[name].wait_recv()
+
+    for k in (1, 3, 2):
+        send(("along", k), rows_buf.at[0, rows_at(0, 0)], rows_buf.at[0, rows_at(0, CHAIN - k)], along[k])
+    to_near(0)
+    to_far(0, 0)
+    to_sibling(0, 0)
+
+    def relay_along(dz):
+        got("along", CHAIN - dz)
+        to_near(dz)
+        to_far(0, dz)
+        to_sibling(0, dz)
+
+    def relay_near(dz):
+        got("near", dz, 0)
+        got("near", dz, 1)
+        to_far(1, dz)
+        to_sibling(1, dz)
+
+    def relay_far(b, dz):
+        got("far", b, dz, 0)
+        got("far", b, dz, 1)
+        to_sibling(2 + b, dz)
+
+    def compute(batch):
+        for dz in range(CHAIN):
+            got("pair", batch, dz)
+        acc_g[...] = jnp.zeros_like(acc_g)
+        acc_u[...] = jnp.zeros_like(acc_u)
+
+        def project(n, carry):
+            at = pl.ds(pl.multiple_of(n * STEP, STEP), STEP)
+            block = rows_buf[batch, :, at]
+            acc_g[...] += jnp.dot(block, wg[at, :], preferred_element_type=jnp.float32)
+            acc_u[...] += jnp.dot(block, wu[at, :], preferred_element_type=jnp.float32)
+            return carry
+
+        lax.fori_loop(0, width // STEP, project, 0)
+        gate = acc_g[...]
+        hid[...] = (jax.nn.silu(gate) * acc_u[...]).astype(jnp.bfloat16)
+        mine = lax.div(me, TGROUP) * 2 + core
+        lanes = lax.broadcasted_iota(jnp.int32, (BATCH, LANES), 1)
+        chosen = (lanes == mine) | (lanes == mine + LANES // 2)
+        tail = rows_buf[batch, :, pl.ds(width, LANES)].astype(jnp.float32)
+        combine = jnp.sum(jnp.where(chosen, tail, 0.0), axis=1, keepdims=True)
+
+        def expand(n, carry):
+            at = pl.ds(pl.multiple_of(n * STEP, STEP), STEP)
+            piece = jnp.dot(hid[...], wd[:, at], preferred_element_type=jnp.float32)
+            part_buf[batch, :, at] = (piece * combine).astype(jnp.bfloat16)
+            return carry
+
+        lax.fori_loop(0, width // STEP, expand, 0)
+        send(("sum", batch), part_buf.at[batch, pl.ds(SIDE, SIDE)], pair_buf.at[batch], sibling)
+
+    def add_rows(batch, dst, src_ref, count):
+        def body(n, carry):
+            at = pl.ds(pl.multiple_of(n * HALF, HALF), HALF)
+            to = pl.ds(pl.multiple_of(dst + n * HALF, HALF), HALF)
+            part_buf[batch, to, :] = (
+                part_buf[batch, to, :].astype(jnp.float32) + src_ref[at, :].astype(jnp.float32)
+            ).astype(jnp.bfloat16)
+            return carry
+
+        lax.fori_loop(0, count, body, 0)
+
+    def sum_pair(batch):
+        got("sum", batch)
+        add_rows(batch, 0, pair_buf.at[batch], SIDE // HALF)
+
+    relay_along(1)
+    relay_near(0)
+    relay_along(3)
+    relay_near(1)
+    relay_along(2)
+    relay_near(3)
+    relay_near(2)
+    for load in loads:
+        load.wait()
+    compute(0)
+    compute(1)
+    for dz in (0, 1, 3, 2):
+        relay_far(0, dz)
+    compute(2)
+    for dz in (0, 1, 3, 2):
+        relay_far(1, dz)
+    sum_pair(2)
+
+    def back_far(b):
+        for dz in (2, 1, 3, 0):
+            for h in range(2):
+                send(
+                    ("back_far", b, dz, h), part_buf.at[2 + b, rows_at(0, dz, h)],
+                    far_buf.at[b, rows_at(0, dz, h)], far[h],
+                )
+
+    back_far(0)
+    compute(3)
+    sum_pair(0)
+    sum_pair(1)
+    sum_pair(3)
+    back_far(1)
+    for b in (0, 1):
+        for dz in (2, 1, 3, 0):
+            got("back_far", b, dz, 0)
+            got("back_far", b, dz, 1)
+            add_rows(b, dz * BLOCK, far_buf.at[b, rows_at(0, dz)], 2)
+            if b == 1:
+                for h in range(2):
+                    send(
+                        ("back_near", dz, h), part_buf.at[1, rows_at(0, dz, h)],
+                        near_buf.at[rows_at(0, dz, h)], near[h],
+                    )
+    for dz in (2, 1, 3, 0):
+        got("back_near", dz, 0)
+        got("back_near", dz, 1)
+        add_rows(0, dz * BLOCK, near_buf.at[rows_at(0, dz)], 2)
+        if dz:
+            send(("home", dz), part_buf.at[0, rows_at(0, dz)], chain_buf.at[dz - 1], along[dz])
+    for dz in (1, 3, 2):
+        got("home", dz)
+    mixture = part_buf[0, pl.ds(0, BLOCK), :].astype(jnp.float32)
+    for dz in range(1, CHAIN):
+        mixture = mixture + chain_buf[dz - 1].astype(jnp.float32)
+    out_ref[...] = (hidden_ref[...].astype(jnp.float32) + mixture).astype(jnp.bfloat16)
+    for copy in sent.values():
+        copy.wait_send()
+
+
+COPIES = 80
+
+
+def per_device_kernel(hidden_rows, norm_gain, expert_ids, capacity, route_probs, w_gate, w_up, w_down):
+    row_count, width = hidden_rows.shape
+    units = w_gate.shape[-1]
+    vmem = pl.BlockSpec(memory_space=pltpu.VMEM)
+    anywhere = pl.BlockSpec(memory_space=pl.ANY)
+    bf16 = jnp.bfloat16
+    return pl.pallas_call(
+        layer_kernel,
+        out_shape=jax.ShapeDtypeStruct((row_count, width), bf16),
+        in_specs=[vmem, vmem, vmem, pl.BlockSpec(memory_space=pltpu.SMEM), vmem, anywhere, anywhere, anywhere],
+        out_specs=vmem,
+        scratch_shapes=[
+            pltpu.VMEM((4, BATCH, width + LANES), bf16),
+            pltpu.VMEM((4, BATCH, width), bf16),
+            pltpu.VMEM((4, SIDE, width), bf16),
+            pltpu.VMEM((2, SIDE, width), bf16),
+            pltpu.VMEM((SIDE, width), bf16),
+            pltpu.VMEM((CHAIN - 1, BLOCK, width), bf16),
+            pltpu.VMEM((width, units), bf16),
+            pltpu.VMEM((width, units), bf16),
+            pltpu.VMEM((units, width), bf16),
+            pltpu.VMEM((BATCH, units), jnp.float32),
+            pltpu.VMEM((BATCH, units), jnp.float32),
+            pltpu.VMEM((BATCH, units), bf16),
+            pltpu.SemaphoreType.DMA((3,)),
+            pltpu.SemaphoreType.DMA((COPIES,)),
+            pltpu.SemaphoreType.DMA((COPIES,)),
+        ],
+        compiler_params=pltpu.CompilerParams(
+            collective_id=0, has_side_effects=True, vmem_limit_bytes=56 * 1024 * 1024
+        ),
+    )(
+        hidden_rows, norm_gain.reshape(1, width), expert_ids, capacity, route_probs,
+        w_gate[0, 0], w_up[0, 0], w_down[0, 0],
+    )
+
+
 def solution(mesh):
     placed = (
         P(("groups", "expert", "replica"), None),
@@ -80,8 +344,10 @@
         P("expert", "replica", None, None),
         P("expert", "replica", None, None),
     )
+    shape = dict(mesh.shape)
+    sliced = (shape["groups"], shape["expert"], shape["replica"]) == (1, 4 * CHAIN, 2)
     return jax.shard_map(
-        per_device,
+        per_device_kernel if sliced else per_device,
         mesh=mesh,
         in_specs=placed,
         out_specs=P(("groups", "expert", "replica"), None),

time: 351 us -> 118 us (0.34)
  the two profiles are of different devices: /device:TPU:0 before, /device:TPU:17 now
where the time goes in v1:
time: 118 us; the launch traced here: 117 us
  Pallas kernels  104 us (88%)
  local copies, waits for them, and re-layouts  12.9 us (11%)
    pallas_call x1, Pallas kernels, per_device_kernel(): pl.pallas_call(layer_kernel, out_shape=jax.ShapeDtypeStruct((row_count, w...  104 us
    unnamed x7, local copies, waits for them, and re-layouts  11.6 us

profile of v1, /device:TPU:17, one launch (start us, length us, event | category | flops | bytes accessed | tf_op | source)
XLA Modules:
  0.0 117.2 jit_solution(4863973456068370077)
XLA Ops:
  0.0 1.3 %reshape.3.gain_ref = f32[1,3584]{1,0:T(1,128)} reshape(f32[3584]{0:T(1024)} %param.9) | data formatting | bytes 28672 | tf_op jit(solution)/shard_map/reshape | solution.py:331
  1.3 1.4 %copy.11.ids_ref = s32[32,2]{1,0:T(8,128)} copy(s32[32,2]{0,1:T(2,128)} %param.10) | data formatting | bytes 512 | tf_op args[2]
  2.7 1.4 %copy.12.probs_ref = f32[32,2]{1,0:T(8,128)} copy(f32[32,2]{0,1:T(2,128)} %param.12) | data formatting | bytes 512 | tf_op args[4]
  4.1 0.0 copy-start
  4.1 4.5 %copy.9 = bf16[1,1,3584,304]{3,2,1,0:T(8,128)(2,1)} copy(bf16[1,1,3584,304]{2,3,1,0:T(8,128)(2,1)} %param.13) | data formatting | bytes 4358144 | tf_op args[5]
  8.6 0.0 copy-done
  8.6 2.7 %copy.10 = bf16[1,1,3584,304]{3,2,1,0:T(8,128)(2,1)} copy(bf16[1,1,3584,304]{2,3,1,0:T(8,128)(2,1)S(1)} %copy-done) | data formatting | bytes 4358144 | tf_op args[6]
  11.3 104.3 %shard_map.82 = bf16[32,3584]{1,0:T(8,128)(2,1)} custom-call(bf16[32,3584]{1,0:T(8,128)(2,1)} %hidden_ref.1, f32[1,3584]{1,0:T(1,128)} %reshape.3.gain_ref, s32[32,2]{1,0:T(8,128)} %copy.11.ids_ref, s32[4]{0:T(128)} %cap_ref.1, f32[32,2]{1,0:T(8,128)} %copy.12.probs_ref, bf16[3584,304]{1,0:T(8,128)(2,1)} %bitcast.3, bf16[3584,304]{1,0:T(8,128)(2,1)} %bitcast.4, ...), custom_call_target="tpu_custom_call" | custom-call | tf_op jit(solution)/shard_map/pallas_call | solution.py:305
  115.6 1.6 %copy.14 = bf16[32,3584]{1,0:T(8,128)(2,1)} copy(bf16[32,3584]{1,0:T(8,128)(2,1)} %shard_map.82) | data formatting | bytes 458752
Async XLA Ops:
  4.1 4.5 %copy-start = (bf16[1,1,3584,304]{2,3,1,0:T(8,128)(2,1)S(1)}, bf16[1,1,3584,304]{2,3,1,0:T(8,128)(2,1)}, u32[]{:S(2)}) copy-start(bf16[1,1,3584,304]{2,3,1,0:T(8,128)(2,1)} %param.14) | copy-start | bytes 6537220

commit v2 on v1

--- a/solution.py
+++ b/solution.py
@@ -87,10 +87,11 @@
 
 def layer_kernel(
     hidden_ref, gain_ref, ids_ref, cap_ref, probs_ref, wg_hbm, wu_hbm, wd_hbm, out_ref,
-    rows_buf, part_buf, pair_buf, far_buf, near_buf, chain_buf, wg, wu, wd, acc_g, acc_u, hid,
+    rows_buf, part_buf, pair_buf, far_buf, near_buf, chain_buf, wgu, wd, acc, hid,
     load_sem, send_sem, recv_sem,
 ):
     width = hidden_ref.shape[1]
+    units = wd.shape[0]
     experts = cap_ref.shape[0]
     me = lax.axis_index("expert")
     core = lax.axis_index("replica")
@@ -104,7 +105,9 @@
 
     loads = [
         pltpu.make_async_copy(src, dst, load_sem.at[n])
-        for n, (src, dst) in enumerate(((wg_hbm, wg), (wu_hbm, wu), (wd_hbm, wd)))
+        for n, (src, dst) in enumerate(
+            ((wg_hbm, wgu.at[pl.ds(0, units)]), (wu_hbm, wgu.at[pl.ds(units, units)]), (wd_hbm, wd))
+        )
     ]
     for load in loads:
         load.start()
@@ -116,11 +119,17 @@
 
     widened = hidden_ref[...].astype(jnp.float32)
     scaling = lax.rsqrt(jnp.mean(widened * widened, axis=-1, keepdims=True) + 1e-05)
-    rows_buf[0, pl.ds(0, BLOCK), pl.ds(0, width)] = (widened * scaling * gain_ref[...]).astype(jnp.bfloat16)
+    rows_buf[0, pl.ds(0, BLOCK), pl.ds(0, width)] = (widened * scaling * gain_ref[...][None, :]).astype(jnp.bfloat16)
     lane = lax.broadcasted_iota(jnp.int32, (BLOCK, LANES), 1)
     label = jnp.where(lane < LANES // 2, lane, lane - LANES // 2)
-    first = ids_ref[:, 0:1] == label
-    second = ids_ref[:, 1:2] == label
+    diagonal = lax.broadcasted_iota(jnp.int32, (BLOCK, BLOCK), 0) == lax.broadcasted_iota(jnp.int32, (BLOCK, BLOCK), 1)
+
+    def column(ref, k):
+        row = ref[k : k + 1, :].astype(jnp.float32)
+        return jnp.sum(jnp.where(diagonal, row, 0.0), axis=1, keepdims=True)
+
+    first = column(ids_ref, 0).astype(jnp.int32) == label
+    second = column(ids_ref, 1).astype(jnp.int32) == label
     named = jnp.where(first | second, 1.0, 0.0)
     earlier = lax.broadcasted_iota(jnp.int32, (BLOCK, BLOCK), 1) < lax.broadcasted_iota(jnp.int32, (BLOCK, BLOCK), 0)
     rank = jnp.dot(
@@ -131,7 +140,7 @@
     limit = jnp.zeros((BLOCK, LANES), jnp.float32)
     for e in range(experts):
         limit = jnp.where(label == e, cap_ref[e].astype(jnp.float32), limit)
-    weight = jnp.where(first, probs_ref[:, 0:1], 0.0) + jnp.where(second, probs_ref[:, 1:2], 0.0)
+    weight = jnp.where(first, column(probs_ref, 0), 0.0) + jnp.where(second, column(probs_ref, 1), 0.0)
     weight = jnp.where(rank < limit, weight, 0.0)
     high = weight.astype(jnp.bfloat16).astype(jnp.float32)
     rows_buf[0, pl.ds(0, BLOCK), pl.ds(width, LANES)] = jnp.where(
@@ -191,19 +200,17 @@
     def compute(batch):
         for dz in range(CHAIN):
             got("pair", batch, dz)
-        acc_g[...] = jnp.zeros_like(acc_g)
-        acc_u[...] = jnp.zeros_like(acc_u)
+        acc[...] = jnp.zeros_like(acc)
 
         def project(n, carry):
             at = pl.ds(pl.multiple_of(n * STEP, STEP), STEP)
-            block = rows_buf[batch, :, at]
-            acc_g[...] += jnp.dot(block, wg[at, :], preferred_element_type=jnp.float32)
-            acc_u[...] += jnp.dot(block, wu[at, :], preferred_element_type=jnp.float32)
+            acc[...] += lax.dot_general(
+                wgu[:, at], rows_buf[batch, :, at], (((1,), (1,)), ((), ())), preferred_element_type=jnp.float32
+            )
             return carry
 
         lax.fori_loop(0, width // STEP, project, 0)
-        gate = acc_g[...]
-        hid[...] = (jax.nn.silu(gate) * acc_u[...]).astype(jnp.bfloat16)
+        hid[...] = jnp.transpose(jax.nn.silu(acc[pl.ds(0, units), :]) * acc[pl.ds(units, units), :]).astype(jnp.bfloat16)
         mine = lax.div(me, TGROUP) * 2 + core
         lanes = lax.broadcasted_iota(jnp.int32, (BATCH, LANES), 1)
         chosen = (lanes == mine) | (lanes == mine + LANES // 2)
@@ -314,11 +321,9 @@
             pltpu.VMEM((2, SIDE, width), bf16),
             pltpu.VMEM((SIDE, width), bf16),
             pltpu.VMEM((CHAIN - 1, BLOCK, width), bf16),
-            pltpu.VMEM((width, units), bf16),
-            pltpu.VMEM((width, units), bf16),
+            pltpu.VMEM((2 * units, width), bf16),
             pltpu.VMEM((units, width), bf16),
-            pltpu.VMEM((BATCH, units), jnp.float32),
-            pltpu.VMEM((BATCH, units), jnp.float32),
+            pltpu.VMEM((2 * units, BATCH), jnp.float32),
             pltpu.VMEM((BATCH, units), bf16),
             pltpu.SemaphoreType.DMA((3,)),
             pltpu.SemaphoreType.DMA((COPIES,)),
@@ -328,8 +333,8 @@
             collective_id=0, has_side_effects=True, vmem_limit_bytes=56 * 1024 * 1024
         ),
     )(
-        hidden_rows, norm_gain.reshape(1, width), expert_ids, capacity, route_probs,
-        w_gate[0, 0], w_up[0, 0], w_down[0, 0],
+        hidden_rows, norm_gain, expert_ids.T, capacity, route_probs.T,
+        w_gate[0, 0].T, w_up[0, 0].T, w_down[0, 0],
     )
 
 

time: 118 us -> 105 us (0.89)
  the two profiles are of different devices: /device:TPU:17 before, /device:TPU:0 now
where the time goes in v2:
time: 105 us; the launch traced here: 103 us
  Pallas kernels  102 us (97%)
  local copies, waits for them, and re-layouts  1.64 us (2%)
    pallas_call x1, Pallas kernels, per_device_kernel(): pl.pallas_call(layer_kernel, out_shape=jax.ShapeDtypeStruct((row_count, w...  102 us

profile of v2, /device:TPU:0, one launch (start us, length us, event | category | flops | bytes accessed | tf_op | source)
XLA Modules:
  0.0 103.2 jit_solution(631675252935259269)
XLA Ops:
  0.0 101.6 %shard_map.82 = bf16[32,3584]{1,0:T(8,128)(2,1)} custom-call(bf16[32,3584]{1,0:T(8,128)(2,1)} %hidden_ref.1, f32[3584]{0:T(1024)} %gain_ref.1, s32[2,32]{1,0:T(2,128)} %bitcast.12, s32[4]{0:T(128)} %cap_ref.1, f32[2,32]{1,0:T(2,128)} %bitcast.13, bf16[304,3584]{1,0:T(8,128)(2,1)} %bitcast.9, bf16[304,3584]{1,0:T(8,128)(2,1)} %bitcast.10, ...), custom_call_target="tpu_custom_call" | custom-call | tf_op jit(solution)/shard_map/pallas_call | solution.py:312
  101.6 1.6 %copy.10 = bf16[32,3584]{1,0:T(8,128)(2,1)} copy(bf16[32,3584]{1,0:T(8,128)(2,1)} %shard_map.82) | data formatting | bytes 458752

commit v3 on v2

--- a/solution.py
+++ b/solution.py
@@ -80,14 +80,14 @@
 STEP = 512
 
 
-def rows_at(dc, dz, h=None):
-    start = dc * SIDE + dz * BLOCK
+def rows_at(core_side, far_side, near_side, h=None):
+    start = core_side * SIDE + far_side * 2 * BLOCK + near_side * BLOCK
     return pl.ds(start, BLOCK) if h is None else pl.ds(start + h * HALF, HALF)
 
 
 def layer_kernel(
     hidden_ref, gain_ref, ids_ref, cap_ref, probs_ref, wg_hbm, wu_hbm, wd_hbm, out_ref,
-    rows_buf, part_buf, pair_buf, far_buf, near_buf, chain_buf, wgu, wd, acc, hid,
+    rows_buf, part_buf, pair_buf, far_buf, near_buf, ring_buf, wgu, wd, acc, hid,
     load_sem, send_sem, recv_sem,
 ):
     width = hidden_ref.shape[1]
@@ -99,7 +99,9 @@
     x_side = {"expert": me + 1 - 2 * lax.rem(me, 2)}
     y_side = {"expert": me + 2 - 4 * lax.rem(lax.div(me, 2), 2)}
     sibling = {"replica": 1 - core}
-    along = [{"expert": lax.rem(me + 4 * k, total)} for k in range(CHAIN)]
+    turn = 4 - 8 * core
+    after = {"expert": lax.rem(me + total + turn, total)}
+    before = {"expert": lax.rem(me + total - turn, total)}
     near = (x_side, y_side)
     far = (y_side, x_side)
 
@@ -113,7 +115,7 @@
         load.start()
 
     barrier = pltpu.get_barrier_semaphore()
-    partners = [x_side, y_side, sibling] + along[1:]
+    partners = [x_side, y_side, sibling, after, before]
     for partner in partners:
         pl.semaphore_signal(barrier, inc=1, device_id=partner, device_id_type=pl.DeviceIdType.MESH)
 
@@ -160,46 +162,41 @@
         copy.start()
         sent[name] = copy
 
-    def to_near(dz):
-        for h in range(2):
-            send(("near", dz, h), rows_buf.at[0, rows_at(0, dz, h)], rows_buf.at[1, rows_at(0, dz, h)], near[h])
-
-    def to_far(b, dz):
-        for h in range(2):
-            send(("far", b, dz, h), rows_buf.at[b, rows_at(0, dz, h)], rows_buf.at[2 + b, rows_at(0, dz, h)], far[h])
-
-    def to_sibling(batch, dz):
-        send(("pair", batch, dz), rows_buf.at[batch, rows_at(0, dz)], rows_buf.at[batch, rows_at(1, dz)], sibling)
-
     def got(*name):
         sent[name].wait_recv()
 
-    for k in (1, 3, 2):
-        send(("along", k), rows_buf.at[0, rows_at(0, 0)], rows_buf.at[0, rows_at(0, CHAIN - k)], along[k])
-    to_near(0)
-    to_far(0, 0)
-    to_sibling(0, 0)
-
-    def relay_along(dz):
-        got("along", CHAIN - dz)
-        to_near(dz)
-        to_far(0, dz)
-        to_sibling(0, dz)
-
-    def relay_near(dz):
-        got("near", dz, 0)
-        got("near", dz, 1)
-        to_far(1, dz)
-        to_sibling(1, dz)
-
-    def relay_far(b, dz):
-        got("far", b, dz, 0)
-        got("far", b, dz, 1)
-        to_sibling(2 + b, dz)
+    def pass_on(s):
+        if s:
+            got("along", s)
+        mine = rows_at(0, 0, 0)
+        if s + 1 < CHAIN:
+            send(("along", s + 1), rows_buf.at[s, mine], rows_buf.at[s + 1, mine], after)
+        for h in range(2):
+            send(("near", s, h), rows_buf.at[s, rows_at(0, 0, 0, h)], rows_buf.at[s, rows_at(0, 0, 1, h)], near[h])
+        for h in range(2):
+            send(("far", s, 0, h), rows_buf.at[s, rows_at(0, 0, 0, h)], rows_buf.at[s, rows_at(0, 1, 0, h)], far[h])
+
+    def share(s, side):
+        send(
+            ("pair", s, side), rows_buf.at[s, pl.ds(side * 2 * BLOCK, 2 * BLOCK)],
+            rows_buf.at[s, pl.ds(SIDE + side * 2 * BLOCK, 2 * BLOCK)], sibling,
+        )
+
+    def relay_near(s):
+        for h in range(2):
+            got("near", s, h)
+            send(("far", s, 1, h), rows_buf.at[s, rows_at(0, 0, 1, h)], rows_buf.at[s, rows_at(0, 1, 1, h)], far[h])
+        share(s, 0)
+
+    def relay_far(s):
+        for b in range(2):
+            for h in range(2):
+                got("far", s, b, h)
+        share(s, 1)
 
     def compute(batch):
-        for dz in range(CHAIN):
-            got("pair", batch, dz)
+        for side in range(2):
+            got("pair", batch, side)
         acc[...] = jnp.zeros_like(acc)
 
         def project(n, carry):
@@ -237,70 +234,73 @@
 
         lax.fori_loop(0, count, body, 0)
 
-    def sum_pair(batch):
-        got("sum", batch)
-        add_rows(batch, 0, pair_buf.at[batch], SIDE // HALF)
-
-    relay_along(1)
+    def sum_pair(s):
+        got("sum", s)
+        add_rows(s, 0, pair_buf.at[s], SIDE // HALF)
+        for b in (1, 0):
+            for h in range(2):
+                send(
+                    ("back_far", s, b, h), part_buf.at[s, rows_at(0, 1, b, h)],
+                    far_buf.at[s, rows_at(0, 0, b, h)], far[h],
+                )
+
+    def sum_far(s):
+        for h in range(2):
+            got("back_far", s, 1, h)
+            add_rows(s, BLOCK + h * HALF, far_buf.at[s, rows_at(0, 0, 1, h)], 1)
+            send(("back_near", s, h), part_buf.at[s, rows_at(0, 0, 1, h)], near_buf.at[s, rows_at(0, 0, 0, h)], near[h])
+        for h in range(2):
+            got("back_far", s, 0, h)
+            add_rows(s, h * HALF, far_buf.at[s, rows_at(0, 0, 0, h)], 1)
+
+    def sum_near(s):
+        for h in range(2):
+            got("back_near", s, h)
+            add_rows(s, h * HALF, near_buf.at[s, rows_at(0, 0, 0, h)], 1)
+        if s != 1:
+            got("home", s)
+            add_rows(s, 0, ring_buf.at[s], 2)
+        if s:
+            last = (s + 1) % CHAIN
+            send(("home", last), part_buf.at[s, rows_at(0, 0, 0)], ring_buf.at[last], after)
+
+    pass_on(0)
     relay_near(0)
-    relay_along(3)
+    pass_on(1)
+    relay_far(0)
     relay_near(1)
-    relay_along(2)
-    relay_near(3)
-    relay_near(2)
+    pass_on(2)
     for load in loads:
         load.wait()
     compute(0)
+    relay_far(1)
+    relay_near(2)
+    pass_on(3)
     compute(1)
-    for dz in (0, 1, 3, 2):
-        relay_far(0, dz)
+    relay_far(2)
+    relay_near(3)
+    sum_pair(1)
     compute(2)
-    for dz in (0, 1, 3, 2):
-        relay_far(1, dz)
+    relay_far(3)
     sum_pair(2)
-
-    def back_far(b):
-        for dz in (2, 1, 3, 0):
-            for h in range(2):
-                send(
-                    ("back_far", b, dz, h), part_buf.at[2 + b, rows_at(0, dz, h)],
-                    far_buf.at[b, rows_at(0, dz, h)], far[h],
-                )
-
-    back_far(0)
+    sum_far(1)
     compute(3)
+    sum_pair(3)
+    sum_near(1)
+    sum_far(2)
     sum_pair(0)
-    sum_pair(1)
-    sum_pair(3)
-    back_far(1)
-    for b in (0, 1):
-        for dz in (2, 1, 3, 0):
-            got("back_far", b, dz, 0)
-            got("back_far", b, dz, 1)
-            add_rows(b, dz * BLOCK, far_buf.at[b, rows_at(0, dz)], 2)
-            if b == 1:
-                for h in range(2):
-                    send(
-                        ("back_near", dz, h), part_buf.at[1, rows_at(0, dz, h)],
-                        near_buf.at[rows_at(0, dz, h)], near[h],
-                    )
-    for dz in (2, 1, 3, 0):
-        got("back_near", dz, 0)
-        got("back_near", dz, 1)
-        add_rows(0, dz * BLOCK, near_buf.at[rows_at(0, dz)], 2)
-        if dz:
-            send(("home", dz), part_buf.at[0, rows_at(0, dz)], chain_buf.at[dz - 1], along[dz])
-    for dz in (1, 3, 2):
-        got("home", dz)
+    sum_near(2)
+    sum_far(3)
+    sum_near(3)
+    sum_far(0)
+    sum_near(0)
     mixture = part_buf[0, pl.ds(0, BLOCK), :].astype(jnp.float32)
-    for dz in range(1, CHAIN):
-        mixture = mixture + chain_buf[dz - 1].astype(jnp.float32)
     out_ref[...] = (hidden_ref[...].astype(jnp.float32) + mixture).astype(jnp.bfloat16)
     for copy in sent.values():
         copy.wait_send()
 
 
-COPIES = 80
+COPIES = 66
 
 
 def per_device_kernel(hidden_rows, norm_gain, expert_ids, capacity, route_probs, w_gate, w_up, w_down):
@@ -318,9 +318,9 @@
             pltpu.VMEM((4, BATCH, width + LANES), bf16),
             pltpu.VMEM((4, BATCH, width), bf16),
             pltpu.VMEM((4, SIDE, width), bf16),
-            pltpu.VMEM((2, SIDE, width), bf16),
-            pltpu.VMEM((SIDE, width), bf16),
-            pltpu.VMEM((CHAIN - 1, BLOCK, width), bf16),
+            pltpu.VMEM((4, 2 * BLOCK, width), bf16),
+            pltpu.VMEM((4, BLOCK, width), bf16),
+            pltpu.VMEM((4, BLOCK, width), bf16),
             pltpu.VMEM((2 * units, width), bf16),
             pltpu.VMEM((units, width), bf16),
             pltpu.VMEM((2 * units, BATCH), jnp.float32),

time: 105 us -> 79 us (0.75); the launches traced: 103 us -> 78.9 us
  Pallas kernels: 102 us -> 77.2 us
    pallas_call x1, Pallas kernels: 102 us -> 77.2 us  [per_device_kernel(): pl.pallas_call(layer_kernel, out_shape=jax.ShapeDtypeStruct((row_count, w...]
where the time goes in v3:
time: 79 us; the launch traced here: 78.9 us
  Pallas kernels  77.2 us (98%)
  local copies, waits for them, and re-layouts  1.64 us (2%)
    pallas_call x1, Pallas kernels, per_device_kernel(): pl.pallas_call(layer_kernel, out_shape=jax.ShapeDtypeStruct((row_count, w...  77.2 us
    unnamed x1, local copies, waits for them, and re-layouts  1.64 us

profile of v3, /device:TPU:0, one launch (start us, length us, event | category | flops | bytes accessed | tf_op | source)
XLA Modules:
  0.0 78.9 jit_solution(16898163173851145663)
XLA Ops:
  0.0 77.2 %shard_map.82 = bf16[32,3584]{1,0:T(8,128)(2,1)} custom-call(bf16[32,3584]{1,0:T(8,128)(2,1)} %hidden_ref.1, f32[3584]{0:T(1024)} %gain_ref.1, s32[2,32]{1,0:T(2,128)} %bitcast.12, s32[4]{0:T(128)} %cap_ref.1, f32[2,32]{1,0:T(2,128)} %bitcast.13, bf16[304,3584]{1,0:T(8,128)(2,1)} %bitcast.9, bf16[304,3584]{1,0:T(8,128)(2,1)} %bitcast.10, ...), custom_call_target="tpu_custom_call" | custom-call | tf_op jit(solution)/shard_map/pallas_call | solution.py:312
  77.2 1.6 %copy.10 = bf16[32,3584]{1,0:T(8,128)(2,1)} copy(bf16[32,3584]{1,0:T(8,128)(2,1)} %shard_map.82) | data formatting | bytes 458752

commit v4 on v3

--- a/solution.py
+++ b/solution.py
@@ -77,12 +77,12 @@
 BLOCK = 2 * HALF
 SIDE = CHAIN * BLOCK
 BATCH = 2 * SIDE
-STEP = 512
-
-
-def rows_at(core_side, far_side, near_side, h=None):
-    start = core_side * SIDE + far_side * 2 * BLOCK + near_side * BLOCK
-    return pl.ds(start, BLOCK) if h is None else pl.ds(start + h * HALF, HALF)
+STEP = 1792
+SPLIT = 2816
+
+
+def rows_at(core_side, far_side, h, near_side, count=HALF):
+    return pl.ds(core_side * SIDE + far_side * 2 * BLOCK + h * BLOCK + near_side * HALF, count)
 
 
 def layer_kernel(
@@ -121,7 +121,9 @@
 
     widened = hidden_ref[...].astype(jnp.float32)
     scaling = lax.rsqrt(jnp.mean(widened * widened, axis=-1, keepdims=True) + 1e-05)
-    rows_buf[0, pl.ds(0, BLOCK), pl.ds(0, width)] = (widened * scaling * gain_ref[...][None, :]).astype(jnp.bfloat16)
+    normed = (widened * scaling * gain_ref[...][None, :]).astype(jnp.bfloat16)
+    for h in range(2):
+        rows_buf[0, rows_at(0, 0, h, 0), pl.ds(0, width)] = normed[h * HALF : (h + 1) * HALF]
     lane = lax.broadcasted_iota(jnp.int32, (BLOCK, LANES), 1)
     label = jnp.where(lane < LANES // 2, lane, lane - LANES // 2)
     diagonal = lax.broadcasted_iota(jnp.int32, (BLOCK, BLOCK), 0) == lax.broadcasted_iota(jnp.int32, (BLOCK, BLOCK), 1)
@@ -145,9 +147,9 @@
     weight = jnp.where(first, column(probs_ref, 0), 0.0) + jnp.where(second, column(probs_ref, 1), 0.0)
     weight = jnp.where(rank < limit, weight, 0.0)
     high = weight.astype(jnp.bfloat16).astype(jnp.float32)
-    rows_buf[0, pl.ds(0, BLOCK), pl.ds(width, LANES)] = jnp.where(
-        lane < LANES // 2, high, weight - high
-    ).astype(jnp.bfloat16)
+    tail = jnp.where(lane < LANES // 2, high, weight - high).astype(jnp.bfloat16)
+    for h in range(2):
+        rows_buf[0, rows_at(0, 0, h, 0), pl.ds(width, LANES)] = tail[h * HALF : (h + 1) * HALF]
 
     pl.semaphore_wait(barrier, len(partners))
 
@@ -165,16 +167,39 @@
     def got(*name):
         sent[name].wait_recv()
 
+    z_first = pl.ds(0, SPLIT)
+    near_first = pl.ds(SPLIT, width + LANES - SPLIT)
+
+    def relay(name, s, src, dst, device, columns, to=None):
+        send(name, rows_buf.at[s, src, columns], rows_buf.at[s if to is None else to, dst, columns], device)
+
     def pass_on(s):
+        for h in range(2):
+            own = rows_at(0, 0, h, 0)
+            if s:
+                got("along", s, h)
+            if s + 1 < CHAIN:
+                relay(("along", s + 1, h), s, own, own, after, z_first, s + 1)
+        for h in range(2):
+            relay(("near", s, h), s, rows_at(0, 0, h, 0), rows_at(0, 0, h, 1), near[h], z_first)
+        for h in range(2):
+            relay(("far", s, 0, h), s, rows_at(0, 0, h, 0), rows_at(0, 1, h, 0), far[h], z_first)
+
+    def start_near():
+        for h in range(2):
+            relay(("near_one", h), 0, rows_at(0, 0, h, 0), rows_at(0, 0, h, 1), near[h], near_first)
+
+    def pass_two(s):
         if s:
-            got("along", s)
-        mine = rows_at(0, 0, 0)
+            got("along_two", s)
+        else:
+            for h in range(2):
+                got("near_one", h)
+        both = pl.ds(0, 2 * BLOCK)
         if s + 1 < CHAIN:
-            send(("along", s + 1), rows_buf.at[s, mine], rows_buf.at[s + 1, mine], after)
-        for h in range(2):
-            send(("near", s, h), rows_buf.at[s, rows_at(0, 0, 0, h)], rows_buf.at[s, rows_at(0, 0, 1, h)], near[h])
-        for h in range(2):
-            send(("far", s, 0, h), rows_buf.at[s, rows_at(0, 0, 0, h)], rows_buf.at[s, rows_at(0, 1, 0, h)], far[h])
+            relay(("along_two", s + 1), s, both, both, after, near_first, s + 1)
+        for h in range(2):
+            relay(("far_two", s, h), s, rows_at(0, 0, h, 0, BLOCK), rows_at(0, 1, h, 0, BLOCK), far[h], near_first)
 
     def share(s, side):
         send(
@@ -185,13 +210,14 @@
     def relay_near(s):
         for h in range(2):
             got("near", s, h)
-            send(("far", s, 1, h), rows_buf.at[s, rows_at(0, 0, 1, h)], rows_buf.at[s, rows_at(0, 1, 1, h)], far[h])
+            relay(("far", s, 1, h), s, rows_at(0, 0, h, 1), rows_at(0, 1, h, 1), far[h], z_first)
         share(s, 0)
 
     def relay_far(s):
-        for b in range(2):
-            for h in range(2):
+        for h in range(2):
+            for b in range(2):
                 got("far", s, b, h)
+            got("far_two", s, h)
         share(s, 1)
 
     def compute(batch):
@@ -223,59 +249,91 @@
         lax.fori_loop(0, width // STEP, expand, 0)
         send(("sum", batch), part_buf.at[batch, pl.ds(SIDE, SIDE)], pair_buf.at[batch], sibling)
 
-    def add_rows(batch, dst, src_ref, count):
+    def add_rows(batch, dst, src_ref, count, columns):
         def body(n, carry):
             at = pl.ds(pl.multiple_of(n * HALF, HALF), HALF)
             to = pl.ds(pl.multiple_of(dst + n * HALF, HALF), HALF)
-            part_buf[batch, to, :] = (
-                part_buf[batch, to, :].astype(jnp.float32) + src_ref[at, :].astype(jnp.float32)
+            part_buf[batch, to, columns] = (
+                part_buf[batch, to, columns].astype(jnp.float32) + src_ref[at, columns].astype(jnp.float32)
             ).astype(jnp.bfloat16)
             return carry
 
         lax.fori_loop(0, count, body, 0)
 
+    last_near = pl.ds(SPLIT, width - SPLIT)
+
+    def give(name, s, src, buf, to, dst, device, columns):
+        send(name, part_buf.at[s, src, columns], buf.at[to, dst, columns], device)
+
     def sum_pair(s):
         got("sum", s)
-        add_rows(s, 0, pair_buf.at[s], SIDE // HALF)
+        add_rows(s, 0, pair_buf.at[s], SIDE // HALF, pl.ds(0, width))
+        for h in range(2):
+            give(
+                ("back_far_two", s, h), s, rows_at(0, 1, h, 0, BLOCK), far_buf, s, rows_at(0, 0, h, 0, BLOCK),
+                far[h], last_near,
+            )
         for b in (1, 0):
             for h in range(2):
-                send(
-                    ("back_far", s, b, h), part_buf.at[s, rows_at(0, 1, b, h)],
-                    far_buf.at[s, rows_at(0, 0, b, h)], far[h],
+                give(("back_far", s, b, h), s, rows_at(0, 1, h, b), far_buf, s, rows_at(0, 0, h, b), far[h], z_first)
+
+    def sum_far(s):
+        for h in range(2):
+            got("back_far_two", s, h)
+            add_rows(s, h * BLOCK, far_buf.at[s, pl.ds(h * BLOCK, BLOCK)], 2, last_near)
+        if s != 1:
+            got("home_two", s)
+            add_rows(s, 0, ring_buf.at[s], 4, last_near)
+        if s:
+            following = (s + 1) % CHAIN
+            both = pl.ds(0, 2 * BLOCK)
+            give(("home_two", following), s, both, ring_buf, following, both, after, last_near)
+        else:
+            for h in range(2):
+                give(
+                    ("back_near_one", h), 0, rows_at(0, 0, h, 1), near_buf, 0, pl.ds(h * HALF, HALF), near[h], last_near
                 )
-
-    def sum_far(s):
         for h in range(2):
             got("back_far", s, 1, h)
-            add_rows(s, BLOCK + h * HALF, far_buf.at[s, rows_at(0, 0, 1, h)], 1)
-            send(("back_near", s, h), part_buf.at[s, rows_at(0, 0, 1, h)], near_buf.at[s, rows_at(0, 0, 0, h)], near[h])
+            add_rows(s, h * BLOCK + HALF, far_buf.at[s, rows_at(0, 0, h, 1)], 1, z_first)
+            give(("back_near", s, h), s, rows_at(0, 0, h, 1), near_buf, s, pl.ds(h * HALF, HALF), near[h], z_first)
         for h in range(2):
             got("back_far", s, 0, h)
-            add_rows(s, h * HALF, far_buf.at[s, rows_at(0, 0, 0, h)], 1)
+            add_rows(s, h * BLOCK, far_buf.at[s, rows_at(0, 0, h, 0)], 1, z_first)
 
     def sum_near(s):
         for h in range(2):
+            own = rows_at(0, 0, h, 0)
             got("back_near", s, h)
-            add_rows(s, h * HALF, near_buf.at[s, rows_at(0, 0, 0, h)], 1)
-        if s != 1:
-            got("home", s)
-            add_rows(s, 0, ring_buf.at[s], 2)
-        if s:
-            last = (s + 1) % CHAIN
-            send(("home", last), part_buf.at[s, rows_at(0, 0, 0)], ring_buf.at[last], after)
-
+            add_rows(s, h * BLOCK, near_buf.at[s, pl.ds(h * HALF, HALF)], 1, z_first)
+            if s != 1:
+                got("home", s, h)
+                add_rows(s, h * BLOCK, ring_buf.at[s, own], 1, z_first)
+            if s:
+                following = (s + 1) % CHAIN
+                give(("home", following, h), s, own, ring_buf, following, own, after, z_first)
+        if s == 0:
+            for h in range(2):
+                got("back_near_one", h)
+                add_rows(s, h * BLOCK, near_buf.at[s, pl.ds(h * HALF, HALF)], 1, last_near)
+
+    start_near()
     pass_on(0)
+    pass_two(0)
     relay_near(0)
     pass_on(1)
+    pass_two(1)
     relay_far(0)
     relay_near(1)
     pass_on(2)
+    pass_two(2)
     for load in loads:
         load.wait()
     compute(0)
     relay_far(1)
     relay_near(2)
     pass_on(3)
+    pass_two(3)
     compute(1)
     relay_far(2)
     relay_near(3)
@@ -283,8 +341,8 @@
     compute(2)
     relay_far(3)
     sum_pair(2)
+    compute(3)
     sum_far(1)
-    compute(3)
     sum_pair(3)
     sum_near(1)
     sum_far(2)
@@ -294,13 +352,15 @@
     sum_near(3)
     sum_far(0)
     sum_near(0)
-    mixture = part_buf[0, pl.ds(0, BLOCK), :].astype(jnp.float32)
-    out_ref[...] = (hidden_ref[...].astype(jnp.float32) + mixture).astype(jnp.bfloat16)
+    for h in range(2):
+        mine = pl.ds(h * HALF, HALF)
+        mixture = part_buf[0, rows_at(0, 0, h, 0), :].astype(jnp.float32)
+        out_ref[mine, :] = (hidden_ref[mine, :].astype(jnp.float32) + mixture).astype(jnp.bfloat16)
     for copy in sent.values():
         copy.wait_send()
 
 
-COPIES = 66
+COPIES = 98
 
 
 def per_device_kernel(hidden_rows, norm_gain, expert_ids, capacity, route_probs, w_gate, w_up, w_down):
@@ -320,7 +380,7 @@
             pltpu.VMEM((4, SIDE, width), bf16),
             pltpu.VMEM((4, 2 * BLOCK, width), bf16),
             pltpu.VMEM((4, BLOCK, width), bf16),
-            pltpu.VMEM((4, BLOCK, width), bf16),
+            pltpu.VMEM((4, 2 * BLOCK, width), bf16),
             pltpu.VMEM((2 * units, width), bf16),
             pltpu.VMEM((units, width), bf16),
             pltpu.VMEM((2 * units, BATCH), jnp.float32),

time: 79 us -> 72.6 us (0.919)
  Pallas kernels: 77.2 us -> 70.8 us
    pallas_call x1, Pallas kernels: 77.2 us -> 70.8 us  [per_device_kernel(): pl.pallas_call(layer_kernel, out_shape=jax.ShapeDtypeStruct((row_count, w...]
where the time goes in v4:
time: 72.6 us; the launch traced here: 72.5 us
  Pallas kernels  70.8 us (98%)
  local copies, waits for them, and re-layouts  1.64 us (2%)
    pallas_call x1, Pallas kernels, per_device_kernel(): pl.pallas_call(layer_kernel, out_shape=jax.ShapeDtypeStruct((row_count, w...  70.8 us
    unnamed x1, local copies, waits for them, and re-layouts  1.64 us

profile of v4, /device:TPU:0, one launch (start us, length us, event | category | flops | bytes accessed | tf_op | source)
XLA Modules:
  0.0 72.5 jit_solution(4134394080855283449)
XLA Ops:
  0.0 70.8 %shard_map.82 = bf16[32,3584]{1,0:T(8,128)(2,1)} custom-call(bf16[32,3584]{1,0:T(8,128)(2,1)} %hidden_ref.1, f32[3584]{0:T(1024)} %gain_ref.1, s32[2,32]{1,0:T(2,128)} %bitcast.12, s32[4]{0:T(128)} %cap_ref.1, f32[2,32]{1,0:T(2,128)} %bitcast.13, bf16[304,3584]{1,0:T(8,128)(2,1)} %bitcast.9, bf16[304,3584]{1,0:T(8,128)(2,1)} %bitcast.10, ...), custom_call_target="tpu_custom_call" | custom-call | tf_op jit(solution)/shard_map/pallas_call | solution.py:372
  70.8 1.6 %copy.10 = bf16[32,3584]{1,0:T(8,128)(2,1)} copy(bf16[32,3584]{1,0:T(8,128)(2,1)} %shard_map.82) | data formatting | bytes 458752

commit v5 on v4

--- a/solution.py
+++ b/solution.py
@@ -182,6 +182,8 @@
                 relay(("along", s + 1, h), s, own, own, after, z_first, s + 1)
         for h in range(2):
             relay(("near", s, h), s, rows_at(0, 0, h, 0), rows_at(0, 0, h, 1), near[h], z_first)
+
+    def pass_far(s):
         for h in range(2):
             relay(("far", s, 0, h), s, rows_at(0, 0, h, 0), rows_at(0, 1, h, 0), far[h], z_first)
 
@@ -240,14 +242,11 @@
         tail = rows_buf[batch, :, pl.ds(width, LANES)].astype(jnp.float32)
         combine = jnp.sum(jnp.where(chosen, tail, 0.0), axis=1, keepdims=True)
 
-        def expand(n, carry):
-            at = pl.ds(pl.multiple_of(n * STEP, STEP), STEP)
+        for n in range(width // STEP):
+            at = pl.ds(n * STEP, STEP)
             piece = jnp.dot(hid[...], wd[:, at], preferred_element_type=jnp.float32)
             part_buf[batch, :, at] = (piece * combine).astype(jnp.bfloat16)
-            return carry
-
-        lax.fori_loop(0, width // STEP, expand, 0)
-        send(("sum", batch), part_buf.at[batch, pl.ds(SIDE, SIDE)], pair_buf.at[batch], sibling)
+            send(("sum", batch, n), part_buf.at[batch, pl.ds(SIDE, SIDE), at], pair_buf.at[batch, :, at], sibling)
 
     def add_rows(batch, dst, src_ref, count, columns):
         def body(n, carry):
@@ -266,8 +265,9 @@
         send(name, part_buf.at[s, src, columns], buf.at[to, dst, columns], device)
 
     def sum_pair(s):
-        got("sum", s)
-        add_rows(s, 0, pair_buf.at[s], SIDE // HALF, pl.ds(0, width))
+        for n in range(width // STEP):
+            got("sum", s, n)
+            add_rows(s, 0, pair_buf.at[s], SIDE // HALF, pl.ds(n * STEP, STEP))
         for h in range(2):
             give(
                 ("back_far_two", s, h), s, rows_at(0, 1, h, 0, BLOCK), far_buf, s, rows_at(0, 0, h, 0, BLOCK),
@@ -320,13 +320,16 @@
     start_near()
     pass_on(0)
     pass_two(0)
+    pass_far(0)
     relay_near(0)
     pass_on(1)
     pass_two(1)
+    pass_far(1)
     relay_far(0)
     relay_near(1)
     pass_on(2)
     pass_two(2)
+    pass_far(2)
     for load in loads:
         load.wait()
     compute(0)
@@ -334,6 +337,7 @@
     relay_near(2)
     pass_on(3)
     pass_two(3)
+    pass_far(3)
     compute(1)
     relay_far(2)
     relay_near(3)
@@ -360,7 +364,7 @@
         copy.wait_send()
 
 
-COPIES = 98
+COPIES = 102
 
 
 def per_device_kernel(hidden_rows, norm_gain, expert_ids, capacity, route_probs, w_gate, w_up, w_down):

time: 72.6 us -> 71.8 us (0.989)
  Pallas kernels: 70.8 us -> 70 us
    pallas_call x1, Pallas kernels: 70.8 us -> 70 us  [per_device_kernel(): pl.pallas_call(layer_kernel, out_shape=jax.ShapeDtypeStruct((row_count, w...]
where the time goes in v5:
time: 71.8 us; the launch traced here: 71.6 us
  Pallas kernels  70 us (97%)
  local copies, waits for them, and re-layouts  1.64 us (2%)
    pallas_call x1, Pallas kernels, per_device_kernel(): pl.pallas_call(layer_kernel, out_shape=jax.ShapeDtypeStruct((row_count, w...  70 us
    unnamed x1, local copies, waits for them, and re-layouts  1.64 us

profile of v5, /device:TPU:0, one launch (start us, length us, event | category | flops | bytes accessed | tf_op | source)
XLA Modules:
  0.0 71.6 jit_solution(16143371115766706946)
XLA Ops:
  0.0 70.0 %shard_map.82 = bf16[32,3584]{1,0:T(8,128)(2,1)} custom-call(bf16[32,3584]{1,0:T(8,128)(2,1)} %hidden_ref.1, f32[3584]{0:T(1024)} %gain_ref.1, s32[2,32]{1,0:T(2,128)} %bitcast.12, s32[4]{0:T(128)} %cap_ref.1, f32[2,32]{1,0:T(2,128)} %bitcast.13, bf16[304,3584]{1,0:T(8,128)(2,1)} %bitcast.9, bf16[304,3584]{1,0:T(8,128)(2,1)} %bitcast.10, ...), custom_call_target="tpu_custom_call" | custom-call | tf_op jit(solution)/shard_map/pallas_call | solution.py:376
  70.0 1.6 %copy.10 = bf16[32,3584]{1,0:T(8,128)(2,1)} copy(bf16[32,3584]{1,0:T(8,128)(2,1)} %shard_map.82) | data formatting | bytes 458752
